TPU v7x, 128 devices: a whole 4x4x4 slice. The times are simulated.
128 devices in a mesh: grp: 4 (over z), seq: 8 (over y_lo, x), rep: 4 (over y_hi, core).
Axes of the slice: x: 4, y: 4 (y_hi: 2, y_lo: 2; y = y_hi * 2 + y_lo), z: 4, core: 2. Of those that a mesh axis runs over, the one named last changes fastest.
Arguments:
- base_hidden: bfloat16 [32, 192, 3072], P(('seq', 'rep'), 'grp'), may hold values from -6 to 6
- base_query: bfloat16 [32, 192, 3072], P(('seq', 'rep'), 'grp'), may hold values from -24 to 24
- base_key: bfloat16 [32, 192, 3072], P(('seq', 'rep'), 'grp'), may hold values from -24 to 24
- base_value: bfloat16 [32, 192, 3072], P(('seq', 'rep'), 'grp'), may hold values from -6 to 6
- base_text_key: bfloat16 [512, 3072], P(None, 'seq'), may hold values from -6 to 6
- base_text_value: bfloat16 [512, 3072], P(None, 'seq'), may hold values from -24 to 24
- base_out_weight: bfloat16 [3072, 3072], P('seq'), may hold values from -0.109375 to 0.109375
- control_hidden: bfloat16 [6144, 3072], P(('seq', 'rep'), 'grp'), may hold values from -6 to 6
- control_query: bfloat16 [6144, 3072], P(('seq', 'rep'), 'grp'), may hold values from -24 to 24
- control_key: bfloat16 [6144, 3072], P(('seq', 'rep'), 'grp'), may hold values from -24 to 24
- control_value: bfloat16 [6144, 3072], P(('seq', 'rep'), 'grp'), may hold values from -6 to 6
- control_text_key: bfloat16 [512, 3072], P(None, 'grp'), may hold values from -6 to 6
- control_text_value: bfloat16 [512, 3072], P(None, 'grp'), may hold values from -24 to 24
- control_out_weight: bfloat16 [3072, 3072], P('grp'), may hold values from -0.109375 to 0.109375
- gate_table: float32 [28, 2, 3072], replicated, may hold values from 0.3 to 3
- control_gain: float32 [3072], replicated, may hold values from 0.3 to 3
- timestep: int32 [1], replicated, may hold values from 0 to 27
- text_length: int32 [1], replicated, may hold values from 128 to 512
Outputs:
- base_out: bfloat16 [32, 192, 3072], P(('seq', 'rep'), 'grp')
All inputs are finite; a program needn't handle non-finite values.
Results may differ from a plain program's by a relative error of at most 0.017.
Values may be sent and summed in bfloat16 or wider, within the bound.
A program may use at most 192 MiB of HBM per device.

v0:
```python
import math

import jax
import jax.numpy as jnp
from jax import lax
from jax.sharding import PartitionSpec as P

HEAD_DIM = 128


def merge_scores(state_now, scores, values):
    running_max, denom_sum, weighted = state_now
    new_max = jnp.maximum(running_max, jnp.max(scores, axis=-1))
    factor = jnp.exp(running_max - new_max)
    weights = jnp.exp(scores - new_max[..., None])
    denom_sum = denom_sum * factor + jnp.sum(weights, axis=-1)
    weighted = weighted * factor[..., None] + jnp.einsum(
        "hqk,khd->hqd", weights.astype(jnp.bfloat16), values, preferred_element_type=jnp.float32
    )
    return (new_max, denom_sum, weighted)


def fold_keys(state_now, key_block, value_block, queries, score_scale):
    scores = (
        jnp.einsum("qhd,khd->hqk", queries, key_block, preferred_element_type=jnp.float32)
        * score_scale
    )
    return merge_scores(state_now, scores, value_block)


def text_state(queries, text_key, text_value, text_length, score_scale):
    row_count, head_count, head_width = queries.shape
    start_state = (
        jnp.full((head_count, row_count), -1e30, jnp.float32),
        jnp.zeros((head_count, row_count), jnp.float32),
        jnp.zeros((head_count, row_count, head_width), jnp.float32),
    )
    scores = (
        jnp.einsum("qhd,khd->hqk", queries, text_key, preferred_element_type=jnp.float32)
        * score_scale
    )
    key_valid = lax.iota(jnp.int32, text_key.shape[0]) < text_length[0]
    scores = jnp.where(key_valid[None, None, :], scores, -1e30)
    return merge_scores(start_state, scores, text_value)


def finish_heads(state_now):
    running_max, denom_sum, weighted = state_now
    attended = weighted / denom_sum[..., None]
    head_count, row_count, head_width = attended.shape
    return (
        attended.transpose(1, 0, 2).reshape(row_count, head_count * head_width).astype(jnp.bfloat16)
    )


def per_device(
    base_hidden,
    base_query,
    base_key,
    base_value,
    base_text_key,
    base_text_value,
    base_out_weight,
    control_hidden,
    control_query,
    control_key,
    control_value,
    control_text_key,
    control_text_value,
    control_out_weight,
    gate_table,
    control_gain,
    timestep,
    text_length,
):
    score_scale = 1.0 / math.sqrt(HEAD_DIM)
    row_count = base_query.shape[1]
    model_width = base_query.shape[2]
    head_total = model_width // HEAD_DIM
    step_gates = lax.dynamic_index_in_dim(gate_table, timestep[0], 0, keepdims=False)
    base_gate = step_gates[0]
    control_gate = step_gates[1]
    base_q = base_query.reshape(row_count, head_total, HEAD_DIM)
    base_k = base_key.reshape(row_count, head_total, HEAD_DIM)
    base_v = base_value.reshape(row_count, head_total, HEAD_DIM)
    swapped_q, swapped_k, swapped_v = (
        lax.all_to_all(base_q, "seq", split_axis=1, concat_axis=0, tiled=True),
        lax.all_to_all(base_k, "seq", split_axis=1, concat_axis=0, tiled=True),
        lax.all_to_all(base_v, "seq", split_axis=1, concat_axis=0, tiled=True),
    )
    local_heads = swapped_q.shape[1]
    base_tk = base_text_key.reshape(base_text_key.shape[0], local_heads, HEAD_DIM)
    base_tv = base_text_value.reshape(base_text_value.shape[0], local_heads, HEAD_DIM)
    base_state = text_state(swapped_q, base_tk, base_tv, text_length, score_scale)
    key_block = (
        lax.all_gather(swapped_k, ("grp", "rep"), axis=0, tiled=True),
        lax.all_gather(swapped_v, ("grp", "rep"), axis=0, tiled=True),
    )
    base_state = fold_keys(base_state, key_block[0], key_block[1], swapped_q, score_scale)
    base_attn = finish_heads(base_state)
    row_block = base_attn
    base_proj = lax.psum_scatter(
        jnp.dot(row_block, base_out_weight, preferred_element_type=jnp.float32).astype(
            jnp.bfloat16
        ),
        "seq",
        scatter_dimension=0,
        tiled=True,
    ).astype(jnp.float32)
    control_rows = control_query.shape[0]
    control_width = control_query.shape[1]
    control_heads = control_width // HEAD_DIM
    control_q = control_query.reshape(control_rows, control_heads, HEAD_DIM)
    control_k = control_key.reshape(control_rows, control_heads, HEAD_DIM)
    control_v = control_value.reshape(control_rows, control_heads, HEAD_DIM)
    control_tk = control_text_key.reshape(control_text_key.shape[0], control_heads, HEAD_DIM)
    control_tv = control_text_value.reshape(control_text_value.shape[0], control_heads, HEAD_DIM)
    control_state = text_state(control_q, control_tk, control_tv, text_length, score_scale)
    key_block = (
        lax.all_gather(control_k, ("seq", "rep"), axis=0, tiled=True),
        lax.all_gather(control_v, ("seq", "rep"), axis=0, tiled=True),
    )
    control_state = fold_keys(control_state, key_block[0], key_block[1], control_q, score_scale)
    control_attn = finish_heads(control_state)
    group_index = lax.axis_index("grp")
    hidden_wide = lax.dynamic_update_slice(
        jnp.zeros((control_rows, model_width), jnp.float32),
        control_hidden.astype(jnp.float32),
        (jnp.zeros((), jnp.int32), group_index * control_width),
    )
    row_block = control_attn
    mixed = jnp.dot(row_block, control_out_weight, preferred_element_type=jnp.float32)
    residual = lax.psum_scatter(
        (control_gain * (hidden_wide + control_gate * mixed)).astype(jnp.bfloat16),
        "grp",
        scatter_dimension=0,
        tiled=True,
    ).astype(jnp.float32)
    mixed_out = base_hidden[0].astype(jnp.float32) + base_gate * base_proj + residual
    return mixed_out.astype(jnp.bfloat16).reshape(1, row_count, model_width)


def solution(mesh):
    placed = (
        P(("seq", "rep"), "grp", None),
        P(("seq", "rep"), "grp", None),
        P(("seq", "rep"), "grp", None),
        P(("seq", "rep"), "grp", None),
        P(None, "seq"),
        P(None, "seq"),
        P("seq", None),
        P(("seq", "rep"), "grp"),
        P(("seq", "rep"), "grp"),
        P(("seq", "rep"), "grp"),
        P(("seq", "rep"), "grp"),
        P(None, "grp"),
        P(None, "grp"),
        P("grp", None),
        P(),
        P(),
        P(),
        P(),
    )
    return jax.shard_map(
        per_device,
        mesh=mesh,
        in_specs=placed,
        out_specs=P(("seq", "rep"), "grp", None),
        check_vma=False,
    )
```

profile of v0, /device:TPU:0, one launch (start us, length us, event | category | flops | bytes accessed | tf_op | source)
XLA Modules:
  0.0 354.3 jit_solution(4047985495185347174)
XLA Ops:
  6.5 1.2 copy.87
  7.8 13.2 %all_to_all.54 = bf16[48,24,128]{2,0,1:T(8,128)(2,1)S(1)} all-to-all(bf16[48,24,128]{2,0,1:T(8,128)(2,1)S(1)} %copy.65), channel_id=1, replica_groups=mesh['grp'=4,'seq'=8,'rep'=4] {'seq'}, dimensions={1} | all-to-all | bytes 589824 | tf_op jit(solution)/shard_map/all_to_all | solution.py:88
  20.9 0.7 copy.66
  21.6 0.0 all-gather.5.cloned.1.call-update
  21.7 0.0 all-gather.7.cloned.1.call-start
  21.8 10.0 %all_to_all.55 = bf16[48,24,128]{2,0,1:T(8,128)(2,1)S(1)} all-to-all(bf16[48,24,128]{2,0,1:T(8,128)(2,1)S(1)} %copy.67), channel_id=1, replica_groups=mesh['grp'=4,'seq'=8,'rep'=4] {'seq'}, dimensions={1} | all-to-all | bytes 589824 | tf_op jit(solution)/shard_map/all_to_all | solution.py:89
  31.9 0.9 copy.69
  32.8 0.0 all-gather.9.cloned.1.call-start
  32.9 0.8 copy_bitcast_fusion.1
  33.6 0.0 all-gather.9.cloned.1.call-update
  33.7 0.0 all-gather.11.cloned.1.call-start
  33.7 1.7 copy_bitcast_fusion
  35.4 0.0 all-gather.11.cloned.1.call-update
  35.5 1.0 copy.86
  36.5 0.8 copy.60
  37.2 4.0 %all-to-all-start = ((bf16[48,24,128]{2,0,1:T(8,128)(2,1)}), bf16[48,24,128]{2,0,1:T(8,128)(2,1)}, u32[]{:S(2)}, u32[]{:S(2)}) async-start(bf16[48,24,128]{2,0,1:T(8,128)(2,1)} %copy.60), calls=%async_computation | async-start | bytes 589824 | tf_op jit(solution)/shard_map/all_to_all | solution.py:87
  41.3 0.0 reduce-scatter.3.cloned.1.call-start
  42.0 0.9 copy.62
  42.9 1.9 copy.64
  44.9 1.4 copy.70
  46.3 2.3 copy.73
  49.2 0.8 constant_dynamic-slice_fusion
  50.1 1.9 fusion.13
  52.0 1.0 copy.61
  53.0 2.9 fusion.12
  55.9 23.9 %all-gather.5.cloned.1.call-done = bf16[6144,3,128]{2,0,1:T(8,128)(2,1)} async-done(((bf16[384,3,128]{2,0,1:T(8,128)(2,1)}), bf16[6144,3,128]{2,0,1:T(8,128)(2,1)}) %all-gather.5.cloned.1.call-update) | async-done | bytes 4718608 | tf_op jit(solution)/shard_map/all_gather | solution.py:96
  79.8 13.6 %multiply_reduce_fusion.1 = (f32[3,384]{1,0:T(4,128)S(1)}, f32[3,384,6144]{2,1,0:T(8,128)}) fusion(bf16[384,3,128]{2,0,1:T(8,128)(2,1)S(1)} %bitcast.157, bf16[6144,3,128]{2,0,1:T(8,128)(2,1)} %all-gather.5.cloned.1.call-done), kind=kOutput, calls=%fused_computation.3 | convolution fusion | flops 1826093952 | bytes 33329664 | tf_op jit(solution)/shard_map/qhd,khd->hqk/dot_general | solution.py:25
  93.4 0.7 fusion.14
  94.1 12.5 %fusion = f32[3,384]{1,0:T(4,128)S(1)} fusion(f32[3,384,6144]{2,1,0:T(8,128)} %get-tuple-element.24, f32[3,384]{1,0:T(4,128)S(1)} %get-tuple-element.16), kind=kLoop, calls=%fused_computation.4 | loop fusion | flops 21232512 | bytes 28320768 | tf_op jit(solution)/shard_map/reduce_sum | solution.py:16
  106.6 32.6 %all-gather.7.cloned.1.call-done = bf16[6144,3,128]{0,2,1:T(8,128)(2,1)} async-done(((bf16[384,3,128]{0,2,1:T(8,128)(2,1)}), bf16[6144,3,128]{0,2,1:T(8,128)(2,1)}) %all-gather.7.cloned.1.call-update) | async-done | bytes 4718608 | tf_op jit(solution)/shard_map/all_gather | solution.py:97
  139.3 13.4 %fusion.26 = f32[384,3,128]{0,2,1:T(8,128)S(1)} fusion(bf16[6144,3,128]{0,2,1:T(8,128)(2,1)} %all-gather.7.cloned.1.call-done, f32[3,384,6144]{2,1,0:T(8,128)} %get-tuple-element.24, f32[3,384]{1,0:T(4,128)S(1)} %get-tuple-element.16), kind=kOutput, calls=%fused_computation.37 | convolution fusion | flops 1833172992 | bytes 33624576 | tf_op jit(solution)/shard_map/hqk,khd->hqd/dot_general | solution.py:17
  152.7 0.8 fusion.32
  153.4 2.8 convolution_convert_fusion
  156.2 0.0 reduce-scatter.3.cloned.1.call-update
  156.3 0.2 reduce-scatter.5.cloned.1.call-start
  156.5 49.8 %all-gather.9.cloned.1.call-done = bf16[6144,6,128]{2,0,1:T(8,128)(2,1)} async-done(((bf16[192,6,128]{2,0,1:T(8,128)(2,1)}), bf16[6144,6,128]{2,0,1:T(8,128)(2,1)}) %all-gather.9.cloned.1.call-update) | async-done | bytes 9437200 | tf_op jit(solution)/shard_map/all_gather | solution.py:120
  206.3 17.2 %multiply_reduce_fusion = (f32[6,192]{1,0:T(8,128)S(1)}, f32[6,192,6144]{2,1,0:T(8,128)}) fusion(bf16[6144,6,128]{2,0,1:T(8,128)(2,1)} %all-gather.9.cloned.1.call-done, bf16[192,768]{1,0:T(8,128)(2,1)S(1)} %copy-done.5), kind=kOutput, calls=%fused_computation.2 | convolution fusion | flops 1826093952 | bytes 38048256 | tf_op jit(solution)/shard_map/qhd,khd->hqk/dot_general | solution.py:25
  223.5 13.0 %fusion.2 = f32[6,192]{1,0:T(8,128)S(1)} fusion(f32[6,192,6144]{2,1,0:T(8,128)} %get-tuple-element.20, f32[6,192]{1,0:T(8,128)S(1)} %get-tuple-element.13), kind=kLoop, calls=%fused_computation.6 | loop fusion | flops 21232512 | bytes 28320768 | tf_op jit(solution)/shard_map/reduce_sum | solution.py:16
  236.5 0.8 fusion.16
  237.3 37.4 %all-gather.11.cloned.1.call-done = bf16[6144,6,128]{2,0,1:T(8,128)(2,1)} async-done(((bf16[192,6,128]{2,0,1:T(8,128)(2,1)}), bf16[6144,6,128]{2,0,1:T(8,128)(2,1)}) %all-gather.11.cloned.1.call-update) | async-done | bytes 9437200 | tf_op jit(solution)/shard_map/all_gather | solution.py:121
  274.7 15.1 %fusion.29 = f32[192,6,128]{2,0,1:T(8,128)S(1)} fusion(bf16[6144,6,128]{2,0,1:T(8,128)(2,1)} %all-gather.11.cloned.1.call-done, f32[6,192,6144]{2,1,0:T(8,128)} %get-tuple-element.20, f32[6,192]{1,0:T(8,128)S(1)} %get-tuple-element.13), kind=kOutput, calls=%fused_computation.38 | convolution fusion | flops 1833172992 | bytes 38343168 | tf_op jit(solution)/shard_map/hqk,khd->hqd/dot_general | solution.py:17
  289.7 1.0 fusion.44
  290.8 3.6 %convolution_multiply_fusion = f32[192,3072]{1,0:T(8,128)S(1)} fusion(bf16[768,3072]{1,0:T(8,128)(2,1)} %param.31, f32[3072]{0:T(1024)S(1)} %bitcast.173, bf16[6,24,8,128]{3,2,1,0:T(8,128)(2,1)S(1)} %fusion.44), kind=kOutput, calls=%fused_computation.15 | convolution fusion | flops 906559488 | bytes 7385088 | tf_op jit(solution)/shard_map/dot_general | solution.py:132
  294.4 0.1 add_dynamic-update-slice_fusion
  294.5 1.2 multiply_convert_fusion
  295.8 24.2 %reduce-scatter.3.cloned.1.call-done = bf16[48,3072]{1,0:T(8,128)(2,1)} async-done(((bf16[384,3072]{1,0:T(8,128)(2,1)}), bf16[48,3072]{1,0:T(8,128)(2,1)}) %reduce-scatter.3.cloned.1.call-update) | async-done | bytes 294928 | tf_op jit(solution)/shard_map/reduce_scatter | solution.py:102
  320.0 25.6 %reduce-scatter.5.cloned.1.call-done = bf16[48,3072]{1,0:T(8,128)(2,1)} async-done(((bf16[192,3072]{1,0:T(8,128)(2,1)}), bf16[48,3072]{1,0:T(8,128)(2,1)}) %reduce-scatter.5.cloned.1.call-update) | async-done | bytes 294928 | tf_op jit(solution)/shard_map/reduce_scatter | solution.py:133
  345.5 1.9 fusion.49
  (41 shorter events, 0.3 us)
Async XLA Ops:
  6.5 146.9 %copy-start = (bf16[384,3072]{1,0:T(8,128)(2,1)S(1)}, bf16[384,3072]{1,0:T(8,128)(2,1)}, u32[]{:S(2)}) copy-start(bf16[384,3072]{1,0:T(8,128)(2,1)} %param.24) | copy-start | bytes 7077892
  6.5 15.2 %copy-start.9 = (bf16[1,48,3072]{2,1,0:T(8,128)(2,1)S(1)}, bf16[1,48,3072]{2,1,0:T(8,128)(2,1)}, u32[]{:S(2)}) copy-start(bf16[1,48,3072]{2,1,0:T(8,128)(2,1)} %param.21) | copy-start | bytes 884740
  6.5 73.3 %all-gather.5.cloned.1.call-start = ((), (), s32[]{:S(2)}) async-start(), calls=%async_computation.5 | async-start | bytes 5013504 | tf_op jit(solution)/shard_map/all_gather | solution.py:96
  7.7 25.1 %copy-start.10 = (bf16[192,768]{1,0:T(8,128)(2,1)S(1)}, bf16[192,768]{1,0:T(8,128)(2,1)}, u32[]{:S(2)}) copy-start(bf16[192,768]{1,0:T(8,128)(2,1)} %param.27) | copy-start | bytes 884740
  21.7 117.6 %all-gather.7.cloned.1.call-start = ((), (), s32[]{:S(2)}) async-start(), calls=%async_computation.6 | async-start | bytes 5013504 | tf_op jit(solution)/shard_map/all_gather | solution.py:97
  31.9 10.1 %copy-start.7 = (bf16[512,384]{1,0:T(8,128)(2,1)S(1)}, bf16[512,384]{1,0:T(8,128)(2,1)}, u32[]{:S(2)}) copy-start(bf16[512,384]{1,0:T(8,128)(2,1)} %param.22) | copy-start | bytes 1179652
  32.8 173.4 %all-gather.9.cloned.1.call-start = ((), (), s32[]{:S(2)}) async-start(), calls=%async_computation.8 | async-start | bytes 9732096 | tf_op jit(solution)/shard_map/all_gather | solution.py:120
  33.7 241.0 %all-gather.11.cloned.1.call-start = ((), (), s32[]{:S(2)}) async-start(), calls=%async_computation.9 | async-start | bytes 9732096 | tf_op jit(solution)/shard_map/all_gather | solution.py:121
  37.2 14.8 %all-to-all-start = ((bf16[48,24,128]{2,0,1:T(8,128)(2,1)}), bf16[48,24,128]{2,0,1:T(8,128)(2,1)}, u32[]{:S(2)}, u32[]{:S(2)}) async-start(bf16[48,24,128]{2,0,1:T(8,128)(2,1)} %copy.60), calls=%async_computation | async-start | bytes 589824 | tf_op jit(solution)/shard_map/all_to_all | solution.py:87
  41.3 278.7 %reduce-scatter.3.cloned.1.call-start = ((), (), s32[]{:S(2)}) async-start(), calls=%async_computation.7 | async-start | bytes 2654208 | tf_op jit(solution)/shard_map/reduce_scatter | solution.py:102
  42.0 8.1 %copy-start.5 = (bf16[192,768]{1,0:T(8,128)(2,1)S(1)}, bf16[192,768]{1,0:T(8,128)(2,1)}, u32[]{:S(2)}) copy-start(bf16[192,768]{1,0:T(8,128)(2,1)} %param.26) | copy-start | bytes 884740
  79.8 13.6 %copy-start.3 = (f32[3,384,512]{2,1,0:T(8,128)S(1)}, f32[3,384,512]{2,1,0:T(8,128)}, u32[]{:S(2)}) copy-start(f32[3,384,512]{2,1,0:T(8,128)} %get-tuple-element.22) | copy-start | bytes 7077892
  106.6 46.0 %copy-start.8 = (bf16[512,384]{0,1:T(8,128)(2,1)S(1)}, bf16[512,384]{0,1:T(8,128)(2,1)}, u32[]{:S(2)}) copy-start(bf16[512,384]{0,1:T(8,128)(2,1)} %copy.64) | copy-start | bytes 1179652
  139.3 13.4 %copy-start.4 = (f32[3,384,512]{2,1,0:T(8,128)S(1)}, f32[3,384,512]{2,1,0:T(8,128)}, u32[]{:S(2)}) copy-start(f32[3,384,512]{2,1,0:T(8,128)} %get-tuple-element.22) | copy-start | bytes 7077892
  156.3 189.3 %reduce-scatter.5.cloned.1.call-start = ((), (), s32[]{:S(2)}) async-start(), calls=%async_computation.10 | async-start | bytes 1474560 | tf_op jit(solution)/shard_map/reduce_scatter | solution.py:133
  223.5 13.0 %copy-start.2 = (f32[6,192,512]{2,1,0:T(8,128)S(1)}, f32[6,192,512]{2,1,0:T(8,128)}, u32[]{:S(2)}) copy-start(f32[6,192,512]{2,1,0:T(8,128)} %get-tuple-element.18) | copy-start | bytes 7077892
  237.3 52.5 %copy-start.6 = (bf16[512,768]{0,1:T(8,128)(2,1)S(1)}, bf16[512,768]{0,1:T(8,128)(2,1)}, u32[]{:S(2)}) copy-start(bf16[512,768]{0,1:T(8,128)(2,1)} %copy.73) | copy-start | bytes 2359300
  290.8 3.6 %copy-start.11 = (bf16[192,768]{1,0:T(8,128)(2,1)S(1)}, bf16[192,768]{1,0:T(8,128)(2,1)}, u32[]{:S(2)}) copy-start(bf16[192,768]{1,0:T(8,128)(2,1)} %param.25) | copy-start | bytes 884740
  290.8 3.7 %copy-start.13 = (f32[3072]{0:T(1024)S(1)}, f32[3072]{0:T(1024)}, u32[]{:S(2)}) copy-start(f32[3072]{0:T(1024)} %param.33) | copy-start | bytes 36868
  294.4 53.1 %copy-start.1 = (bf16[384,3072]{1,0:T(8,128)(2,1)S(1)}, bf16[384,3072]{1,0:T(8,128)(2,1)}, u32[]{:S(2)}) copy-start(bf16[384,3072]{1,0:T(8,128)(2,1)} %param.24) | copy-start | bytes 7077892
  294.5 51.0 %copy-start.12 = (bf16[1,48,3072]{2,1,0:T(8,128)(2,1)S(1)}, bf16[1,48,3072]{2,1,0:T(8,128)(2,1)}, u32[]{:S(2)}) copy-start(bf16[1,48,3072]{2,1,0:T(8,128)(2,1)} %param.18) | copy-start | bytes 884740
Sparse Core Ops, SparseCore 0:
  21.8 58.0 all-gather.4
  82.2 57.0 all-gather.6
  140.9 65.2 all-gather.8
  207.8 66.8 all-gather.10
  276.9 43.0 reduce-scatter.2
  322.3 23.2 reduce-scatter.4
where the time goes:
time: 355 us; the launch traced here: 354 us
  waiting for transfers between devices  194 us (55%)
  matrix products  72.2 us (20%)
  other arithmetic  30.2 us (9%)
  blocking collectives  23.2 us (7%)
  local copies, waits for them, and re-layouts  15.6 us (4%)
  between operations  15.1 us (4%)
  starting transfers between devices  4.44 us (1%)
    all_gather x1, waiting for transfers between devices, per_device(): lax.all_gather(control_k, ('seq', 'rep'), axis=0, tiled=True)  49.8 us
    all_gather x1, waiting for transfers between devices, per_device(): lax.all_gather(control_v, ('seq', 'rep'), axis=0, tiled=True)  37.4 us
    all_gather x1, waiting for transfers between devices, per_device(): lax.all_gather(swapped_v, ('grp', 'rep'), axis=0, tiled=True)  32.6 us
    dot_general x2, matrix products, fold_keys(): jnp.einsum('qhd,khd->hqk', queries, key_block, preferred_element_type=jnp...  30.8 us
    dot_general x4, matrix products, merge_scores(): jnp.einsum('hqk,khd->hqd', weights.astype(jnp.bfloat16), values, preferre...  30.2 us
    reduce_sum x4, other arithmetic, merge_scores(): denom_sum = denom_sum * factor + jnp.sum(weights, axis=-1)  26.9 us
    reduce_scatter x1, waiting for transfers between devices, per_device(): lax.psum_scatter((control_gain * (hidden_wide + control_gate * mixed)).as...  25.6 us
    reduce_scatter x1, waiting for transfers between devices, per_device(): lax.psum_scatter(jnp.dot(row_block, base_out_weight, preferred_element_ty...  24.2 us
  transfers between devices with their start and end apart: 7, of which 6 were waited for; matrix products, arithmetic and copies ran while one was open for 32% of the time, Pallas kernels for 0%

commit v1 on v0

v1 whole, which is shorter than its diff:
```python
import math

import jax
import jax.numpy as jnp
from jax import lax
from jax.experimental import pallas as pl
from jax.experimental.pallas import tpu as pltpu
from jax.sharding import PartitionSpec as P

HD = 128
NH = 3
OWN = 768
TXH = 256
NB = OWN // 192
KA = TXH + 2 * OWN
KALL = TXH + 4 * OWN
ROWS = 384
CH = 768
C2 = math.log2(math.e) / math.sqrt(HD)
NT = (((1,), (1,)), ((), ()))
MESH = pl.DeviceIdType.MESH


def remote(src, dst, ssem, rsem, dev):
    return pltpu.make_async_remote_copy(
        src_ref=src, dst_ref=dst, send_sem=ssem, recv_sem=rsem, device_id=dev, device_id_type=MESH
    )


def wait_bytes(ref, sem):
    pltpu.make_async_copy(ref, ref, sem).wait()


def kernel(
    tl, bh, bq, bk, bv, btk, btv, wb, ch, cq, ck, cv, ctk, ctv, wc, gates, gain, out,
    Q, K, V, M, L, A, PO, PS, RO, RS, O, OG, WX, WC, HID, SB, SC, RB, RC,
    s1_recv, s1_base, s1_ctl, ex_send, ex_recv, q_send, q_recv, p_send, p_recv,
    g_send, g_recv, w_send, w_recv, r_send, r_recv, loc,
):
    z = lax.axis_index("grp")
    seq = lax.axis_index("seq")
    rep = lax.axis_index("rep")
    x, yl = lax.rem(seq, 4), seq // 4
    yh, c = rep // 2, lax.rem(rep, 2)
    y = yh * 2 + yl

    def dev(xx, yy, zz, cc):
        return {"grp": zz, "seq": lax.rem(yy, 2) * 4 + xx, "rep": (yy // 2) * 2 + cc}

    sib = dev(x, y, z, 1 - c)
    pos = (1 - yh) * z + yh * x
    pa = pos + 1 - 2 * lax.rem(pos, 2)
    pb = lax.rem(pos + 3 - 2 * lax.rem(pos, 2), 4)
    dev_a = dev(yh * pa + (1 - yh) * x, y, (1 - yh) * pa + yh * z, c)
    dev_b = dev(yh * pb + (1 - yh) * x, y, (1 - yh) * pb + yh * z, c)
    thalf = pos // 2

    w_loc = [
        pltpu.make_async_copy(wc, WC, loc.at[0]),
        pltpu.make_async_copy(wb, WX.at[pl.ds(pl.multiple_of(yl * 384, 128), 384)], loc.at[1]),
        pltpu.make_async_copy(ch, HID, loc.at[2]),
    ]

    def text_copies(h, is_base):
        rows = pl.ds(pl.multiple_of(thalf * TXH, TXH), TXH)
        if is_base:
            cols = pl.ds(h * HD, HD)
            srcs = (btk, btv)
        else:
            cols = pl.ds(pl.multiple_of(yl * 384 + h * HD, HD), HD)
            srcs = (ctk, ctv)
        return [
            pltpu.make_async_copy(srcs[i].at[rows, cols], (K, V)[i].at[h, pl.ds(0, TXH)], loc.at[3 + i * NH + h])
            for i in range(2)
        ]

    @pl.when(yh == 0)
    def _():
        for h in range(NH):
            for cp in text_copies(h, True):
                cp.start()

    @pl.when(yh == 1)
    def _():
        for h in range(NH):
            for cp in text_copies(h, False):
                cp.start()

    barrier = pltpu.get_barrier_semaphore()
    peers = [dev(lax.rem(x + i % 4, 4), lax.rem(y + i // 4, 4), z, c) for i in range(1, 16)]
    peers += [dev(x, y, lax.rem(z + i, 4), c) for i in range(1, 4)] + [sib]
    for d in peers:
        pl.semaphore_signal(barrier, inc=1, device_id=d, device_id_type=MESH)
    pl.semaphore_wait(barrier, len(peers))

    base_rows = pl.multiple_of((y * 4 + x) * 48, 16)
    ctl_rows = pl.multiple_of(y * 192, 16)
    arrays = ((bk, ck, K, TXH), (bq, cq, Q, 0), (bv, cv, V, TXH))
    for h in range(NH):
        for a, (bsrc, csrc, dst, off) in enumerate(arrays):
            for i in range(8):
                s = lax.rem(seq + i, 8)
                src = bsrc.at[0, :, pl.ds(pl.multiple_of(s * 384 + h * HD, HD), HD)]
                to = dst.at[h, pl.ds(off + base_rows, 48)]
                cp = remote(src, to, s1_base.at[a, h], s1_recv.at[a, h], {"grp": z, "seq": s, "rep": c})
                if i:
                    cp.start()
                else:
                    pl.when(yh == 1)(cp.start)
                    pl.when(yh == 0)(pltpu.make_async_copy(src, to, s1_recv.at[a, h]).start)
            for i in range(2):
                b = lax.rem(yl + i, 2)
                src = csrc.at[:, pl.ds(pl.multiple_of(b * 384 + h * HD, HD), HD)]
                to = dst.at[h, pl.ds(off + ctl_rows, 192)]
                cp = remote(src, to, s1_ctl.at[a, h], s1_recv.at[a, h], {"grp": z, "seq": b * 4 + x, "rep": 2 + c})
                if i:
                    cp.start()
                else:
                    pl.when(yh == 0)(cp.start)
                    pl.when(yh == 1)(pltpu.make_async_copy(src, to, s1_recv.at[a, h]).start)
    for cp in w_loc:
        cp.start()

    kv = ((0, K), (2, V))

    def exchange(i, h, k):
        buf = kv[i][1]
        lo = TXH + (0, 0, 2 * OWN)[k]
        to = TXH + (OWN, 2 * OWN, 3 * OWN)[k]
        return remote(
            buf.at[h, pl.ds(lo, OWN)], buf.at[h, pl.ds(to, OWN)],
            ex_send.at[i, h, k], ex_recv.at[i, h, k], (sib, dev_a, sib)[k],
        )

    def exchange_q(h):
        return remote(Q.at[h, pl.ds(0, OWN)], Q.at[h, pl.ds(OWN, OWN)], q_send.at[h], q_recv.at[h], dev_b)

    def pass_on(h):
        wait_bytes(K.at[h, pl.ds(TXH, OWN)], s1_recv.at[0, h])
        exchange(0, h, 1).start()
        exchange(0, h, 0).start()
        wait_bytes(Q.at[h, pl.ds(0, OWN)], s1_recv.at[1, h])
        exchange_q(h).start()
        wait_bytes(V.at[h, pl.ds(TXH, OWN)], s1_recv.at[2, h])
        exchange(1, h, 1).start()
        exchange(1, h, 0).start()

    def pass_second(h):
        for i in range(2):
            exchange(i, h, 1).wait_recv()
            exchange(i, h, 2).start()

    text_ok = lax.broadcasted_iota(jnp.int32, (ROWS, TXH), 1) + thalf * TXH < tl[0]

    def scores(h, r, lo, n):
        s = lax.dot_general(
            Q[h, pl.ds(r, ROWS)], K[h, pl.ds(lo, n)], NT, preferred_element_type=jnp.float32
        )
        if lo == 0:
            s = jnp.concatenate([jnp.where(text_ok, s[:, :TXH], -1e30), s[:, TXH:]], axis=1)
        return s

    def fold(h, r, s, lo, n):
        rows = pl.ds(r, ROWS)
        top = jnp.broadcast_to(jnp.max(s, axis=1, keepdims=True), (ROWS, HD))
        if lo:
            old = M[h, rows]
            top = jnp.maximum(old, top)
            f = jnp.exp2((old - top) * C2)
        M[h, rows] = top
        w = jnp.exp2((s - top[:, :1]) * C2)
        part = w[:, :HD]
        for i in range(1, n // HD):
            part = part + w[:, i * HD:(i + 1) * HD]
        got = jnp.dot(w.astype(jnp.bfloat16), V[h, pl.ds(lo, n)], preferred_element_type=jnp.float32)
        if lo:
            L[h, rows] = L[h, rows] * f + part
            A[h, rows] = A[h, rows] * f + got
        else:
            L[h, rows] = part
            A[h, rows] = got

    def tiles(h, starts, lo, n):
        s = scores(h, starts[0], lo, n)
        for i, r in enumerate(starts):
            later = scores(h, starts[i + 1], lo, n) if i + 1 < len(starts) else None
            fold(h, r, s, lo, n)
            s = later

    def send_part(h):
        return [
            remote(PO.at[h], RO.at[h], p_send.at[0, h], p_recv.at[0, h], dev_b),
            remote(PS.at[h], RS.at[h], p_send.at[1, h], p_recv.at[1, h], dev_b),
        ]

    def phase_a(h):
        for i in range(2):
            exchange(i, h, 0).wait_recv()
            wait_bytes((K, V)[i].at[h, pl.ds(0, TXH)], loc.at[3 + i * NH + h])
        exchange_q(h).wait_recv()
        tiles(h, (0, 384, 768, 1152), 0, KA)

    def phase_b(h):
        for i in range(2):
            exchange(i, h, 2).wait_recv()
        tiles(h, (768, 1152, 0, 384), KA, 2 * OWN)
        for i in range(OWN // HD):
            rows = pl.ds(OWN + i * HD, HD)
            total = jnp.broadcast_to(jnp.sum(L[h, rows], axis=1, keepdims=True), (HD, HD))
            PO[h, pl.ds(i * HD, HD)] = (A[h, rows] / total).astype(jnp.bfloat16)
            PS[h, pl.ds(i, 1)] = (M[h, rows] * C2 + jnp.log2(total)).T[:1]
        for i in range(OWN // HD, 8):
            PS[h, pl.ds(i, 1)] = jnp.zeros((1, HD), jnp.float32)
        for cp in send_part(h):
            cp.start()

    def give(h, i):
        to = lax.rem(y + i, 4)
        src = O.at[h, pl.ds(pl.multiple_of(to * 192, 16), 192)]
        dst = OG.at[yh, :, pl.ds(pl.multiple_of(yl * 384 + h * HD, HD), HD)]
        if i == 0:
            return pltpu.make_async_copy(src, dst, g_recv.at[yh])
        return remote(src, dst, g_send.at[h, i], g_recv.at[yh], dev(x, to, z, c))

    def merge(h):
        for cp in send_part(h):
            cp.wait_recv()
        for i in range(OWN // HD):
            rows = pl.ds(i * HD, HD)
            total = jnp.broadcast_to(jnp.sum(L[h, rows], axis=1, keepdims=True), (HD, HD))
            mine = M[h, rows] * C2 + jnp.log2(total)
            theirs = jnp.broadcast_to(RS[h, pl.ds(i, 1)], (HD, HD)).T
            top = jnp.maximum(mine, theirs)
            u, v = jnp.exp2(mine - top), jnp.exp2(theirs - top)
            value = A[h, rows] * (u / total) + RO[h, rows].astype(jnp.float32) * v
            O[h, rows] = (value / (u + v)).astype(jnp.bfloat16)
        for i in range(4):
            give(h, i).start()

    w_half = pl.ds(pl.multiple_of(c * 192, 16), 192)
    w_cp = remote(
        wb.at[w_half], WX.at[pl.ds(pl.multiple_of(yl * 384 + c * 192, 16), 192)],
        w_send.at[0], w_recv.at[0], dev(x, lax.rem(y + 3 + 2 * c, 4), z, c),
    )
    w_got = WX.at[pl.ds(pl.multiple_of((1 - yl) * 384 + c * 192, 16), 192)]
    w_sib = WX.at[pl.ds(pl.multiple_of((1 - yl) * 384 + (1 - c) * 192, 16), 192)]
    w_fwd = remote(w_got, w_got, w_send.at[1], w_recv.at[1], sib)

    pass_on(0)
    phase_a(0)
    pass_on(1)
    phase_a(1)
    pass_second(0)
    pass_on(2)
    w_cp.start()
    phase_b(0)
    phase_a(2)
    pass_second(1)
    merge(0)
    phase_b(1)
    pass_second(2)
    merge(1)
    phase_b(2)
    wait_bytes(w_got, w_recv.at[0])
    w_fwd.start()
    merge(2)

    def scatter(k, n, i):
        cols = pl.ds(n * CH, CH)
        if k == 0:
            to = lax.rem(x + i, 4)
            return remote(
                SB.at[pl.ds(pl.multiple_of(to * 48, 16), 48), cols], RB.at[i - 1, :, cols],
                r_send.at[k, n, i - 1], r_recv.at[k, n], dev(to, y, z, c),
            )
        to = lax.rem(z + i, 4)
        return remote(
            SC.at[pl.ds(pl.multiple_of(to * 48, 16), 48), cols], RC.at[i - 1, :, cols],
            r_send.at[k, n, i - 1], r_recv.at[k, n], dev(x, y, to, c),
        )

    for cp in w_loc:
        cp.wait()
    wait_bytes(w_sib, w_recv.at[1])
    wait_bytes(OG.at[0], g_recv.at[0])
    wait_bytes(OG.at[1], g_recv.at[1])
    for n in range(3072 // CH):
        cols = pl.ds(n * CH, CH)
        got = jnp.dot(OG[0], WX[:, cols], preferred_element_type=jnp.float32)
        SB[:, cols] = (gates[0:1, cols] * got).astype(jnp.bfloat16)
        for i in range(1, 4):
            scatter(0, n, i).start()
        got = gates[1:2, cols] * jnp.dot(OG[1], WC[:, cols], preferred_element_type=jnp.float32)
        got = got + jnp.where(z == n, HID[...].astype(jnp.float32), 0.0)
        SC[:, cols] = (gain[0:1, cols] * got).astype(jnp.bfloat16)
        for i in range(1, 4):
            scatter(1, n, i).start()
    for n in range(3072 // CH):
        cols = pl.ds(n * CH, CH)
        wait_bytes(RB.at[:, :, cols], r_recv.at[0, n])
        wait_bytes(RC.at[:, :, cols], r_recv.at[1, n])
        total = bh[0, :, cols].astype(jnp.float32)
        total = total + SB[pl.ds(pl.multiple_of(x * 48, 16), 48), cols].astype(jnp.float32)
        total = total + SC[pl.ds(pl.multiple_of(z * 48, 16), 48), cols].astype(jnp.float32)
        for i in range(3):
            total = total + RB[i, :, cols].astype(jnp.float32) + RC[i, :, cols].astype(jnp.float32)
        out[:, cols] = total.astype(jnp.bfloat16)

    for h in range(NH):
        for a in range(3):
            @pl.when(yh == 0)
            def _():
                wait_bytes(K.at[h, pl.ds(0, 7 * 48)], s1_base.at[a, h])
                wait_bytes(K.at[h, pl.ds(0, 384)], s1_ctl.at[a, h])

            @pl.when(yh == 1)
            def _():
                wait_bytes(K.at[h, pl.ds(0, 8 * 48)], s1_base.at[a, h])
                wait_bytes(K.at[h, pl.ds(0, 192)], s1_ctl.at[a, h])
        for i in range(2):
            for k in range(3):
                exchange(i, h, k).wait_send()
        exchange_q(h).wait_send()
        for cp in send_part(h):
            cp.wait_send()
        for i in range(1, 4):
            give(h, i).wait_send()
    w_cp.wait_send()
    w_fwd.wait_send()
    for n in range(3072 // CH):
        for k in range(2):
            for i in range(1, 4):
                scatter(k, n, i).wait_send()


def per_device(
    base_hidden, base_query, base_key, base_value, base_text_key, base_text_value, base_out_weight,
    control_hidden, control_query, control_key, control_value, control_text_key, control_text_value,
    control_out_weight, gate_table, control_gain, timestep, text_length,
):
    gates = lax.dynamic_index_in_dim(gate_table, timestep[0], 0, keepdims=False)
    bf, f32 = jnp.bfloat16, jnp.float32
    vm, hbm = pl.BlockSpec(memory_space=pltpu.VMEM), pl.BlockSpec(memory_space=pl.ANY)
    dma = pltpu.SemaphoreType.DMA
    out = pl.pallas_call(
        kernel,
        out_shape=jax.ShapeDtypeStruct((48, 3072), bf),
        in_specs=[pl.BlockSpec(memory_space=pltpu.SMEM), vm] + [hbm] * 13 + [vm, vm],
        out_specs=vm,
        scratch_shapes=[
            pltpu.VMEM((NH, 2 * OWN, HD), bf),
            pltpu.VMEM((NH, KALL, HD), bf),
            pltpu.VMEM((NH, KALL, HD), bf),
            pltpu.VMEM((NH, 2 * OWN, HD), f32),
            pltpu.VMEM((NH, 2 * OWN, HD), f32),
            pltpu.VMEM((NH, 2 * OWN, HD), f32),
            pltpu.VMEM((NH, OWN, HD), bf),
            pltpu.VMEM((NH, 8, HD), f32),
            pltpu.VMEM((NH, OWN, HD), bf),
            pltpu.VMEM((NH, 8, HD), f32),
            pltpu.VMEM((NH, OWN, HD), bf),
            pltpu.VMEM((2, 192, 768), bf),
            pltpu.VMEM((768, 3072), bf),
            pltpu.VMEM((768, 3072), bf),
            pltpu.VMEM((192, 768), bf),
            pltpu.VMEM((192, 3072), bf),
            pltpu.VMEM((192, 3072), bf),
            pltpu.VMEM((3, 48, 3072), bf),
            pltpu.VMEM((3, 48, 3072), bf),
            dma((3, NH)), dma((3, NH)), dma((3, NH)),
            dma((2, NH, 3)), dma((2, NH, 3)), dma((NH,)), dma((NH,)),
            dma((2, NH)), dma((2, NH)), dma((NH, 4)), dma((2,)),
            dma((2,)), dma((2,)), dma((2, 4, 3)), dma((2, 4)), dma((9,)),
        ],
        compiler_params=pltpu.CompilerParams(
            collective_id=0, has_side_effects=True, vmem_limit_bytes=56 * 2**20
        ),
        cost_estimate=pl.CostEstimate(flops=10**10, bytes_accessed=3 * 10**7, transcendentals=16 * 10**6),
    )(
        text_length, base_hidden, base_query, base_key, base_value, base_text_key, base_text_value,
        base_out_weight, control_hidden, control_query, control_key, control_value, control_text_key,
        control_text_value, control_out_weight, gates, control_gain.reshape(1, -1),
    )
    return out.reshape(1, 48, 3072)


def solution(mesh):
    rows, cols = P(("seq", "rep"), "grp", None), P(("seq", "rep"), "grp")
    placed = (
        rows, rows, rows, rows, P(None, "seq"), P(None, "seq"), P("seq", None),
        cols, cols, cols, cols, P(None, "grp"), P(None, "grp"), P("grp", None),
        P(), P(), P(), P(),
    )
    return jax.shard_map(per_device, mesh=mesh, in_specs=placed, out_specs=rows, check_vma=False)
```

time: 355 us -> 101 us (0.28)
  waiting for transfers between devices: 194 us -> 0 us
  Pallas kernels: 0 us -> 97 us
  matrix products: 72.2 us -> 0 us
  other arithmetic: 30.2 us -> 0 us
  blocking collectives: 23.2 us -> 0 us
  between operations: 15.1 us -> 1.39 us
  local copies, waits for them, and re-layouts: 15.6 us -> 2.32 us
  starting transfers between devices: 4.44 us -> 0 us
    all_gather x4 -> x0, waiting for transfers between devices: 144 us -> none  [the longest x1 49.8 us: per_device(): lax.all_gather(control_k, ('seq', 'rep'), axis=0, tiled=True)]
    pallas_call x0 -> x1, Pallas kernels: none -> 97 us  [per_device(): pl.pallas_call(kernel, out_shape=jax.ShapeDtypeStruct((48, 3072), bf), in...]
    dot_general x10 -> x0, matrix products: 72.2 us -> none  [the longest x2 30.8 us: fold_keys(): jnp.einsum('qhd,khd->hqk', queries, key_block, preferred_element_type=jnp...]
    reduce_scatter x2 -> x0, waiting for transfers between devices: 49.7 us -> none  [the longest x1 25.6 us: per_device(): lax.psum_scatter((control_gain * (hidden_wide + control_gate * mixed)).as...]
    reduce_sum x4 -> x0, other arithmetic: 26.9 us -> none  [merge_scores(): denom_sum = denom_sum * factor + jnp.sum(weights, axis=-1)]
    all_to_all x2 -> x0, blocking collectives: 23.2 us -> none  [the longest x1 13.2 us: per_device(): lax.all_to_all(base_k, 'seq', split_axis=1, concat_axis=0, tiled=True)]
    unnamed x35 -> x3, local copies, waits for them, and re-layouts: 8.84 us -> 1.7 us
    all_to_all x1 -> x0, starting transfers between devices: 4.05 us -> none  [per_device(): lax.all_to_all(base_q, 'seq', split_axis=1, concat_axis=0, tiled=True)]
  transfers between devices with their start and end apart: 7 -> 0, of which waited for: 6 -> 0; matrix products, arithmetic and copies ran while one was open for 32% -> 0% of each run, Pallas kernels for 0% -> 0%
where the time goes in v1:
time: 101 us
  Pallas kernels  97 us (96%)
  local copies, waits for them, and re-layouts  2.32 us (2%)
  between operations  1.39 us (1%)
    pallas_call x1, Pallas kernels, per_device(): pl.pallas_call(kernel, out_shape=jax.ShapeDtypeStruct((48, 3072), bf), in...  97 us

profile of v1, /device:TPU:0, one launch (start us, length us, event | category | flops | bytes accessed | tf_op | source)
XLA Modules:
  0.0 100.8 jit_solution(3659285267071665627)
XLA Ops:
  0.0 0.0 copy-start
  1.4 0.0 copy-done
  1.4 0.6 dynamic-slice_bitcast_fusion.gates
  2.0 97.0 %shard_map.172 = bf16[48,3072]{1,0:T(8,128)(2,1)} custom-call(s32[1]{0:T(128)S(6)} %copy.21.tl, bf16[1,48,3072]{2,1,0:T(8,128)(2,1)} %bh.1, bf16[1,48,3072]{2,1,0:T(8,128)(2,1)} %bq.1, bf16[1,48,3072]{2,1,0:T(8,128)(2,1)} %bk.1, bf16[1,48,3072]{2,1,0:T(8,128)(2,1)} %bv.1, bf16[512,384]{1,0:T(8,128)(2,1)} %btk.1, bf16[512,384]{1,0:T(8,128)(2,1)} %btv.1, ...), custom_call_target="tpu_custom_call" | custom-call | flops 10000000000 | bytes 30000000 | tf_op jit(solution)/shard_map/pallas_call | solution.py:345
  99.1 1.7 %copy.22 = bf16[1,48,3072]{2,1,0:T(8,128)(2,1)} copy(bf16[1,48,3072]{2,1,0:T(8,128)(2,1)} %bitcast.8) | data formatting | bytes 589824
Async XLA Ops:
  0.0 1.4 %copy-start = (f32[28,2,3072]{2,1,0:T(2,128)S(1)}, f32[28,2,3072]{2,1,0:T(2,128)}, u32[]{:S(2)}) copy-start(f32[28,2,3072]{2,1,0:T(2,128)} %param.32) | copy-start | bytes 2064388

commit v2 on v1

v2 whole, which is shorter than its diff:
```python
import math

import jax
import jax.numpy as jnp
from jax import lax
from jax.experimental import pallas as pl
from jax.experimental.pallas import tpu as pltpu
from jax.sharding import PartitionSpec as P

HD = 128
NH = 3
OWN = 768
TXH = 256
KA = TXH + 2 * OWN
KALL = TXH + 4 * OWN
ROWS = 384
PARTS = ((0, 16), (16, 32))
CH = 768
C2 = math.log2(math.e) / math.sqrt(HD)
NT = (((1,), (1,)), ((), ()))
MESH = pl.DeviceIdType.MESH


def remote(src, dst, ssem, rsem, dev):
    return pltpu.make_async_remote_copy(
        src_ref=src, dst_ref=dst, send_sem=ssem, recv_sem=rsem, device_id=dev, device_id_type=MESH
    )


def wait_bytes(ref, sem):
    pltpu.make_async_copy(ref, ref, sem).wait()


def kernel(
    tl, ts, bh, bq, bk, bv, btk, btv, wb, ch, cq, ck, cv, ctk, ctv, wc, table, gain, out,
    Q, K, V, M, L, A, PO, PS, RO, RS, O, OG0, OG1, WX, WC, HID, GT, SB0, SB1, SC0, SC1, RB0, RB1, RC0, RC1,
    s1_recv, s1_base, s1_ctl, ex_send, ex_recv, q_send, q_recv, p_send, p_recv,
    g_send, g_recv, w_send, w_recv, r_send, r_recv, loc,
):
    z = lax.axis_index("grp")
    seq = lax.axis_index("seq")
    rep = lax.axis_index("rep")
    x, yl = lax.rem(seq, 4), seq // 4
    yh, c = rep // 2, lax.rem(rep, 2)
    y = yh * 2 + yl

    def dev(xx, yy, zz, cc):
        return {"grp": zz, "seq": lax.rem(yy, 2) * 4 + xx, "rep": (yy // 2) * 2 + cc}

    sib = dev(x, y, z, 1 - c)
    pos = (1 - yh) * z + yh * x
    pa = pos + 1 - 2 * lax.rem(pos, 2)
    pb = lax.rem(pos + 3 - 2 * lax.rem(pos, 2), 4)
    dev_a = dev(yh * pa + (1 - yh) * x, y, (1 - yh) * pa + yh * z, c)
    dev_b = dev(yh * pb + (1 - yh) * x, y, (1 - yh) * pb + yh * z, c)
    thalf = pos // 2

    w_loc = [
        pltpu.make_async_copy(wc, WC, loc.at[0]),
        pltpu.make_async_copy(wb, WX.at[pl.ds(pl.multiple_of(yl * 384, 128), 384)], loc.at[1]),
        pltpu.make_async_copy(ch, HID, loc.at[2]),
        pltpu.make_async_copy(table, GT, loc.at[9]),
    ]

    def text_copies(h, is_base):
        rows = pl.ds(pl.multiple_of(thalf * TXH, TXH), TXH)
        if is_base:
            cols = pl.ds(h * HD, HD)
            srcs = (btk, btv)
        else:
            cols = pl.ds(pl.multiple_of(yl * 384 + h * HD, HD), HD)
            srcs = (ctk, ctv)
        return [
            pltpu.make_async_copy(srcs[i].at[rows, cols], (K, V)[i].at[h, pl.ds(0, TXH)], loc.at[3 + i * NH + h])
            for i in range(2)
        ]

    @pl.when(yh == 0)
    def _():
        for h in range(NH):
            for cp in text_copies(h, True):
                cp.start()

    @pl.when(yh == 1)
    def _():
        for h in range(NH):
            for cp in text_copies(h, False):
                cp.start()

    barrier = pltpu.get_barrier_semaphore()
    peers = [dev(lax.rem(x + i % 4, 4), lax.rem(y + i // 4, 4), z, c) for i in range(1, 16)]
    peers += [dev(x, y, lax.rem(z + i, 4), c) for i in range(1, 4)] + [sib]
    for d in peers:
        pl.semaphore_signal(barrier, inc=1, device_id=d, device_id_type=MESH)
    pl.semaphore_wait(barrier, len(peers))

    base_rows = pl.multiple_of((y * 4 + x) * 48, 16)
    ctl_rows = pl.multiple_of(y * 192, 16)
    arrays = ((bk, ck, K, TXH), (bq, cq, Q, 0), (bv, cv, V, TXH))
    def part_rows(p, block):
        first, count = PARTS[p]
        return pl.ds(pl.multiple_of(first * 16 + block * count, 16), count)

    def stage1(h):
        for a, (bsrc, csrc, dst, off) in enumerate(arrays):
            sem = s1_recv.at[a, h]
            for i in range(2):
                b = lax.rem(yl + i, 2)
                cols = pl.ds(pl.multiple_of(b * 384 + h * HD, HD), HD)
                if a == 1:
                    pieces = [
                        (csrc.at[pl.ds(q * 48 + PARTS[p][0], PARTS[p][1]), cols], dst.at[h, part_rows(p, y * 4 + q)])
                        for q in range(4) for p in range(2)
                    ]
                else:
                    pieces = [(csrc.at[:, cols], dst.at[h, pl.ds(off + ctl_rows, 192)])]
                for src, to in pieces:
                    cp = remote(src, to, s1_ctl.at[a, h], sem, {"grp": z, "seq": b * 4 + x, "rep": 2 + c})
                    if i:
                        cp.start()
                    else:
                        pl.when(yh == 0)(cp.start)
                        pl.when(yh == 1)(pltpu.make_async_copy(src, to, sem).start)
            for i in range(8):
                s = lax.rem(seq + i, 8)
                cols = pl.ds(pl.multiple_of(s * 384 + h * HD, HD), HD)
                if a == 1:
                    pieces = [
                        (bsrc.at[0, pl.ds(*PARTS[p]), cols], dst.at[h, part_rows(p, y * 4 + x)]) for p in range(2)
                    ]
                else:
                    pieces = [(bsrc.at[0, :, cols], dst.at[h, pl.ds(off + base_rows, 48)])]
                for src, to in pieces:
                    cp = remote(src, to, s1_base.at[a, h], sem, {"grp": z, "seq": s, "rep": c})
                    if i:
                        cp.start()
                    else:
                        pl.when(yh == 1)(cp.start)
                        pl.when(yh == 0)(pltpu.make_async_copy(src, to, sem).start)

    stage1(0)
    for cp in w_loc:
        cp.start()

    kv = ((0, K), (2, V))

    def exchange(i, h, k):
        buf = kv[i][1]
        lo = TXH + (0, 0, 2 * OWN)[k]
        to = TXH + (OWN, 2 * OWN, 3 * OWN)[k]
        return remote(
            buf.at[h, pl.ds(lo, OWN)], buf.at[h, pl.ds(to, OWN)],
            ex_send.at[i, h, k], ex_recv.at[i, h, k], (sib, dev_a, sib)[k],
        )

    def exchange_q(h):
        return remote(Q.at[h, pl.ds(0, OWN)], Q.at[h, pl.ds(OWN, OWN)], q_send.at[h], q_recv.at[h], dev_b)

    def pass_on(h):
        wait_bytes(K.at[h, pl.ds(TXH, OWN)], s1_recv.at[0, h])
        exchange(0, h, 1).start()
        exchange(0, h, 0).start()
        if h + 1 < NH:
            stage1(h + 1)
        wait_bytes(Q.at[h, pl.ds(0, OWN)], s1_recv.at[1, h])
        exchange_q(h).start()
        wait_bytes(V.at[h, pl.ds(TXH, OWN)], s1_recv.at[2, h])
        exchange(1, h, 1).start()
        exchange(1, h, 0).start()

    def pass_second(h):
        for i in range(2):
            exchange(i, h, 1).wait_recv()
            exchange(i, h, 2).start()

    text_ok = lax.broadcasted_iota(jnp.int32, (ROWS, TXH), 1) + thalf * TXH < tl[0]

    def scores(h, r, size, lo, n):
        s = lax.dot_general(
            Q[h, pl.ds(r, size)], K[h, pl.ds(lo, n)], NT, preferred_element_type=jnp.float32
        )
        if lo == 0:
            s = jnp.concatenate([jnp.where(text_ok, s[:, :TXH], -1e30), s[:, TXH:]], axis=1)
        return s

    def fold(h, r, size, s, lo, n):
        rows = pl.ds(r, size)
        top = jnp.broadcast_to(jnp.max(s, axis=1, keepdims=True), (size, HD))
        if lo:
            old = M[h, rows]
            top = jnp.maximum(old, top)
            f = jnp.exp2((old - top) * C2)
        M[h, rows] = top
        w = jnp.exp2((s - top[:, :1]) * C2)
        part = w[:, :HD]
        for i in range(1, n // HD):
            part = part + w[:, i * HD:(i + 1) * HD]
        got = jnp.dot(w.astype(jnp.bfloat16), V[h, pl.ds(lo, n)], preferred_element_type=jnp.float32)
        if lo:
            L[h, rows] = L[h, rows] * f + part
            A[h, rows] = A[h, rows] * f + got
        else:
            L[h, rows] = part
            A[h, rows] = got

    def tiles(h, todo, lo, n):
        s = scores(h, *todo[0][:2], lo, n)
        for i, (r, size, then) in enumerate(todo):
            later = scores(h, *todo[i + 1][:2], lo, n) if i + 1 < len(todo) else None
            fold(h, r, size, s, lo, n)
            if then is not None:
                then()
            s = later

    def part_span(p):
        return PARTS[p][0] * 16, PARTS[p][1] * 16

    def send_part(h, p):
        rows = pl.ds(*part_span(p))
        return [
            remote(PO.at[h, rows], RO.at[h, rows], p_send.at[0, h, p], p_recv.at[0, h, p], dev_b),
            remote(PS.at[h, p], RS.at[h, p], p_send.at[1, h, p], p_recv.at[1, h, p], dev_b),
        ]

    def log_sum(h, rows):
        total = jnp.broadcast_to(jnp.sum(L[h, rows], axis=1, keepdims=True), (HD, HD))
        return total, M[h, rows] * C2 + jnp.log2(total)

    def hand_over(h, p):
        first, count = part_span(p)
        for i in range(count // HD):
            rows = pl.ds(OWN + first + i * HD, HD)
            total, both = log_sum(h, rows)
            PO[h, pl.ds(first + i * HD, HD)] = (A[h, rows] / total).astype(jnp.bfloat16)
            PS[h, p, pl.ds(i, 1)] = both.T[:1]
        for i in range(count // HD, 8):
            PS[h, p, pl.ds(i, 1)] = jnp.zeros((1, HD), jnp.float32)
        for cp in send_part(h, p):
            cp.start()

    def phase_a(h):
        for i in range(2):
            exchange(i, h, 0).wait_recv()
            wait_bytes((K, V)[i].at[h, pl.ds(0, TXH)], loc.at[3 + i * NH + h])
        near, far = [(0, ROWS, None), (ROWS, ROWS, None)], [(OWN, ROWS, None), (OWN + ROWS, ROWS, None)]
        if h == 0:
            tiles(h, near, 0, KA)
            exchange_q(h).wait_recv()
            tiles(h, far, 0, KA)
        else:
            exchange_q(h).wait_recv()
            tiles(h, near + far, 0, KA)

    def phase_b(h):
        for i in range(2):
            exchange(i, h, 2).wait_recv()

        def over():
            for p in range(2):
                hand_over(h, p)

        if h + 1 < NH:
            todo = [(OWN, ROWS, None), (OWN + ROWS, ROWS, over), (0, ROWS, None), (ROWS, ROWS, None)]
        else:
            todo = [(OWN + part_span(p)[0], part_span(p)[1], lambda p=p: hand_over(h, p)) for p in range(2)]
            todo += [(*part_span(p), None) for p in range(2)]
        tiles(h, todo, KA, 2 * OWN)

    OG = (OG0, OG1)

    def give(h, p, i):
        to = lax.rem(y + i, 4)
        first, count = PARTS[p]
        src = O.at[h, pl.ds(pl.multiple_of(first * 16 + to * 4 * count, 16), 4 * count)]
        dst = OG[p].at[yh, :, pl.ds(pl.multiple_of(yl * 384 + h * HD, HD), HD)]
        if i == 0:
            return pltpu.make_async_copy(src, dst, g_recv.at[p, yh])
        return remote(src, dst, g_send.at[h, p, i], g_recv.at[p, yh], dev(x, to, z, c))

    def merge(h, p):
        for cp in send_part(h, p):
            cp.wait_recv()
        first, count = part_span(p)
        for i in range(count // HD):
            rows = pl.ds(first + i * HD, HD)
            total, mine = log_sum(h, rows)
            theirs = jnp.broadcast_to(RS[h, p, pl.ds(i, 1)], (HD, HD)).T
            top = jnp.maximum(mine, theirs)
            u, v = jnp.exp2(mine - top), jnp.exp2(theirs - top)
            value = A[h, rows] * (u / total) + RO[h, rows].astype(jnp.float32) * v
            O[h, rows] = (value / (u + v)).astype(jnp.bfloat16)
        for i in range(4):
            give(h, p, i).start()

    w_half = pl.ds(pl.multiple_of(c * 192, 16), 192)
    w_cp = remote(
        wb.at[w_half], WX.at[pl.ds(pl.multiple_of(yl * 384 + c * 192, 16), 192)],
        w_send.at[0], w_recv.at[0], dev(x, lax.rem(y + 3 + 2 * c, 4), z, c),
    )
    w_got = WX.at[pl.ds(pl.multiple_of((1 - yl) * 384 + c * 192, 16), 192)]
    w_sib = WX.at[pl.ds(pl.multiple_of((1 - yl) * 384 + (1 - c) * 192, 16), 192)]
    w_fwd = remote(w_got, w_got, w_send.at[1], w_recv.at[1], sib)

    pass_on(0)
    phase_a(0)
    pass_on(1)
    pass_second(0)
    phase_b(0)
    pass_on(2)
    w_cp.start()
    phase_a(1)
    pass_second(1)
    phase_b(1)
    merge(0, 0)
    merge(0, 1)
    phase_a(2)
    pass_second(2)
    wait_bytes(w_got, w_recv.at[0])
    w_fwd.start()
    merge(1, 0)
    merge(1, 1)
    phase_b(2)
    merge(2, 0)
    merge(2, 1)

    S = ((SB0, SC0), (SB1, SC1))
    R = ((RB0, RC0), (RB1, RC1))

    def scatter(p, k, n, i):
        cols = pl.ds(n * CH, CH)
        count = PARTS[p][1]
        to = lax.rem((x, z)[k] + i, 4)
        return remote(
            S[p][k].at[pl.ds(pl.multiple_of(to * count, 16), count), cols], R[p][k].at[i - 1, :, cols],
            r_send.at[p, k, n, i - 1], r_recv.at[p, k, n], dev(to, y, z, c) if k == 0 else dev(x, y, to, c),
        )

    for cp in w_loc:
        cp.wait()
    wait_bytes(w_sib, w_recv.at[1])
    step = ts[0]
    for p in range(2):
        first, count = PARTS[p]
        wait_bytes(OG[p].at[0], g_recv.at[p, 0])
        wait_bytes(OG[p].at[1], g_recv.at[p, 1])
        hidden = jnp.concatenate([HID[pl.ds(q * 48 + first, count)] for q in range(4)], axis=0).astype(jnp.float32)
        for n in range(3072 // CH):
            cols = pl.ds(n * CH, CH)
            got = jnp.dot(OG[p][0], WX[:, cols], preferred_element_type=jnp.float32)
            S[p][0][:, cols] = (GT[step, 0:1, cols] * got).astype(jnp.bfloat16)
            for i in range(1, 4):
                scatter(p, 0, n, i).start()
            got = GT[step, 1:2, cols] * jnp.dot(OG[p][1], WC[:, cols], preferred_element_type=jnp.float32)
            got = got + jnp.where(z == n, hidden, 0.0)
            S[p][1][:, cols] = (gain[0:1, cols] * got).astype(jnp.bfloat16)
            for i in range(1, 4):
                scatter(p, 1, n, i).start()
    for p in range(2):
        first, count = PARTS[p]
        for n in range(3072 // CH):
            cols = pl.ds(n * CH, CH)
            total = bh[0, pl.ds(first, count), cols].astype(jnp.float32)
            for k in range(2):
                wait_bytes(R[p][k].at[:, :, cols], r_recv.at[p, k, n])
                own = pl.ds(pl.multiple_of((x, z)[k] * count, 16), count)
                total = total + S[p][k][own, cols].astype(jnp.float32)
                for i in range(3):
                    total = total + R[p][k][i, :, cols].astype(jnp.float32)
            out[pl.ds(first, count), cols] = total.astype(jnp.bfloat16)

    for h in range(NH):
        for a in range(3):
            @pl.when(yh == 0)
            def _():
                wait_bytes(K.at[h, pl.ds(0, 7 * 48)], s1_base.at[a, h])
                wait_bytes(K.at[h, pl.ds(0, 384)], s1_ctl.at[a, h])

            @pl.when(yh == 1)
            def _():
                wait_bytes(K.at[h, pl.ds(0, 8 * 48)], s1_base.at[a, h])
                wait_bytes(K.at[h, pl.ds(0, 192)], s1_ctl.at[a, h])
        for i in range(2):
            for k in range(3):
                exchange(i, h, k).wait_send()
        exchange_q(h).wait_send()
        for p in range(2):
            for cp in send_part(h, p):
                cp.wait_send()
            for i in range(1, 4):
                give(h, p, i).wait_send()
    w_cp.wait_send()
    w_fwd.wait_send()
    for n in range(3072 // CH):
        for p in range(2):
            for k in range(2):
                for i in range(1, 4):
                    scatter(p, k, n, i).wait_send()


def per_device(
    base_hidden, base_query, base_key, base_value, base_text_key, base_text_value, base_out_weight,
    control_hidden, control_query, control_key, control_value, control_text_key, control_text_value,
    control_out_weight, gate_table, control_gain, timestep, text_length,
):
    bf, f32 = jnp.bfloat16, jnp.float32
    vm, hbm = pl.BlockSpec(memory_space=pltpu.VMEM), pl.BlockSpec(memory_space=pl.ANY)
    dma = pltpu.SemaphoreType.DMA
    out = pl.pallas_call(
        kernel,
        out_shape=jax.ShapeDtypeStruct((48, 3072), bf),
        in_specs=[pl.BlockSpec(memory_space=pltpu.SMEM)] * 2 + [vm] + [hbm] * 14 + [vm],
        out_specs=vm,
        scratch_shapes=[
            pltpu.VMEM((NH, 2 * OWN, HD), bf),
            pltpu.VMEM((NH, KALL, HD), bf),
            pltpu.VMEM((NH, KALL, HD), bf),
            pltpu.VMEM((NH, 2 * OWN, HD), f32),
            pltpu.VMEM((NH, 2 * OWN, HD), f32),
            pltpu.VMEM((NH, 2 * OWN, HD), f32),
            pltpu.VMEM((NH, OWN, HD), bf),
            pltpu.VMEM((NH, 2, 8, HD), f32),
            pltpu.VMEM((NH, OWN, HD), bf),
            pltpu.VMEM((NH, 2, 8, HD), f32),
            pltpu.VMEM((NH, OWN, HD), bf),
            pltpu.VMEM((2, 64, 768), bf),
            pltpu.VMEM((2, 128, 768), bf),
            pltpu.VMEM((768, 3072), bf),
            pltpu.VMEM((768, 3072), bf),
            pltpu.VMEM((192, 768), bf),
            pltpu.VMEM((28, 2, 3072), f32),
            pltpu.VMEM((64, 3072), bf),
            pltpu.VMEM((128, 3072), bf),
            pltpu.VMEM((64, 3072), bf),
            pltpu.VMEM((128, 3072), bf),
            pltpu.VMEM((3, 16, 3072), bf),
            pltpu.VMEM((3, 32, 3072), bf),
            pltpu.VMEM((3, 16, 3072), bf),
            pltpu.VMEM((3, 32, 3072), bf),
            dma((3, NH)), dma((3, NH)), dma((3, NH)),
            dma((2, NH, 3)), dma((2, NH, 3)), dma((NH,)), dma((NH,)),
            dma((2, NH, 2)), dma((2, NH, 2)), dma((NH, 2, 4)), dma((2, 2)),
            dma((2,)), dma((2,)), dma((2, 2, 4, 3)), dma((2, 2, 4)), dma((10,)),
        ],
        compiler_params=pltpu.CompilerParams(
            collective_id=0, has_side_effects=True, vmem_limit_bytes=56 * 2**20
        ),
        cost_estimate=pl.CostEstimate(flops=10**10, bytes_accessed=3 * 10**7, transcendentals=16 * 10**6),
    )(
        text_length, timestep, base_hidden, base_query, base_key, base_value, base_text_key, base_text_value,
        base_out_weight, control_hidden, control_query, control_key, control_value, control_text_key,
        control_text_value, control_out_weight, gate_table, control_gain.reshape(1, -1),
    )
    return out.reshape(1, 48, 3072)


def solution(mesh):
    rows, cols = P(("seq", "rep"), "grp", None), P(("seq", "rep"), "grp")
    placed = (
        rows, rows, rows, rows, P(None, "seq"), P(None, "seq"), P("seq", None),
        cols, cols, cols, cols, P(None, "grp"), P(None, "grp"), P("grp", None),
        P(), P(), P(), P(),
    )
    return jax.shard_map(per_device, mesh=mesh, in_specs=placed, out_specs=rows, check_vma=False)
```

time: 101 us -> 83.3 us (0.82); the launches traced: 101 us -> 82 us
  Pallas kernels: 97 us -> 79 us
    pallas_call x1, Pallas kernels: 97 us -> 79 us  [per_device(): pl.pallas_call(kernel, out_shape=jax.ShapeDtypeStruct((48, 3072), bf), in...]
where the time goes in v2:
time: 83.3 us; the launch traced here: 82 us
  Pallas kernels  79 us (95%)
  local copies, waits for them, and re-layouts  1.69 us (2%)
  between operations  1.31 us (2%)
    pallas_call x1, Pallas kernels, per_device(): pl.pallas_call(kernel, out_shape=jax.ShapeDtypeStruct((48, 3072), bf), in...  79 us
    unnamed x1, local copies, waits for them, and re-layouts  1.69 us

profile of v2, /device:TPU:0, one launch (start us, length us, event | category | flops | bytes accessed | tf_op | source)
XLA Modules:
  0.0 82.0 jit_solution(2561924633239441751)
XLA Ops:
  1.3 79.0 %shard_map.172 = bf16[48,3072]{1,0:T(8,128)(2,1)} custom-call(s32[1]{0:T(128)S(6)} %copy.21.tl, s32[1]{0:T(128)S(6)} %copy.20.ts, bf16[1,48,3072]{2,1,0:T(8,128)(2,1)} %bh.1, bf16[1,48,3072]{2,1,0:T(8,128)(2,1)} %bq.1, bf16[1,48,3072]{2,1,0:T(8,128)(2,1)} %bk.1, bf16[1,48,3072]{2,1,0:T(8,128)(2,1)} %bv.1, bf16[512,384]{1,0:T(8,128)(2,1)} %btk.1, ...), custom_call_target="tpu_custom_call" | custom-call | flops 10000000000 | bytes 30000000 | tf_op jit(solution)/shard_map/pallas_call | solution.py:408
  80.3 1.7 %copy.22 = bf16[1,48,3072]{2,1,0:T(8,128)(2,1)} copy(bf16[1,48,3072]{2,1,0:T(8,128)(2,1)} %bitcast.2) | data formatting | bytes 589824

commit v3 on v2

--- a/solution.py
+++ b/solution.py
@@ -17,6 +17,7 @@
 PARTS = ((0, 16), (16, 32))
 CH = 768
 C2 = math.log2(math.e) / math.sqrt(HD)
+BLOCK = ((0, KA), (KA, 2 * OWN))
 NT = (((1,), (1,)), ((), ()))
 MESH = pl.DeviceIdType.MESH
 
@@ -53,7 +54,8 @@
     pb = lax.rem(pos + 3 - 2 * lax.rem(pos, 2), 4)
     dev_a = dev(yh * pa + (1 - yh) * x, y, (1 - yh) * pa + yh * z, c)
     dev_b = dev(yh * pb + (1 - yh) * x, y, (1 - yh) * pb + yh * z, c)
-    thalf = pos // 2
+    kv_dev, q_dev = (dev_a, dev_a, dev_b), (dev_b, dev_b, dev_a)
+    thalf = (pos // 2, pos // 2, lax.rem(pos + 1, 4) // 2)
 
     w_loc = [
         pltpu.make_async_copy(wc, WC, loc.at[0]),
@@ -63,7 +65,7 @@
     ]
 
     def text_copies(h, is_base):
-        rows = pl.ds(pl.multiple_of(thalf * TXH, TXH), TXH)
+        rows = pl.ds(pl.multiple_of(thalf[h] * TXH, TXH), TXH)
         if is_base:
             cols = pl.ds(h * HD, HD)
             srcs = (btk, btv)
@@ -101,44 +103,45 @@
         first, count = PARTS[p]
         return pl.ds(pl.multiple_of(first * 16 + block * count, 16), count)
 
-    def stage1(h):
-        for a, (bsrc, csrc, dst, off) in enumerate(arrays):
-            sem = s1_recv.at[a, h]
-            for i in range(2):
-                b = lax.rem(yl + i, 2)
-                cols = pl.ds(pl.multiple_of(b * 384 + h * HD, HD), HD)
-                if a == 1:
-                    pieces = [
-                        (csrc.at[pl.ds(q * 48 + PARTS[p][0], PARTS[p][1]), cols], dst.at[h, part_rows(p, y * 4 + q)])
-                        for q in range(4) for p in range(2)
-                    ]
+    def stage1(h, a):
+        bsrc, csrc, dst, off = arrays[a]
+        sem = s1_recv.at[a, h]
+        for i in range(2):
+            b = lax.rem(yl + i, 2)
+            cols = pl.ds(pl.multiple_of(b * 384 + h * HD, HD), HD)
+            if a == 1:
+                pieces = [
+                    (csrc.at[pl.ds(q * 48 + PARTS[p][0], PARTS[p][1]), cols], dst.at[h, part_rows(p, y * 4 + q)])
+                    for q in range(4) for p in range(2)
+                ]
+            else:
+                pieces = [(csrc.at[:, cols], dst.at[h, pl.ds(off + ctl_rows, 192)])]
+            for src, to in pieces:
+                cp = remote(src, to, s1_ctl.at[a, h], sem, {"grp": z, "seq": b * 4 + x, "rep": 2 + c})
+                if i:
+                    cp.start()
                 else:
-                    pieces = [(csrc.at[:, cols], dst.at[h, pl.ds(off + ctl_rows, 192)])]
-                for src, to in pieces:
-                    cp = remote(src, to, s1_ctl.at[a, h], sem, {"grp": z, "seq": b * 4 + x, "rep": 2 + c})
-                    if i:
-                        cp.start()
-                    else:
-                        pl.when(yh == 0)(cp.start)
-                        pl.when(yh == 1)(pltpu.make_async_copy(src, to, sem).start)
-            for i in range(8):
-                s = lax.rem(seq + i, 8)
-                cols = pl.ds(pl.multiple_of(s * 384 + h * HD, HD), HD)
-                if a == 1:
-                    pieces = [
-                        (bsrc.at[0, pl.ds(*PARTS[p]), cols], dst.at[h, part_rows(p, y * 4 + x)]) for p in range(2)
-                    ]
+                    pl.when(yh == 0)(cp.start)
+                    pl.when(yh == 1)(pltpu.make_async_copy(src, to, sem).start)
+        for i in range(8):
+            s = lax.rem(seq + i, 8)
+            cols = pl.ds(pl.multiple_of(s * 384 + h * HD, HD), HD)
+            if a == 1:
+                pieces = [
+                    (bsrc.at[0, pl.ds(*PARTS[p]), cols], dst.at[h, part_rows(p, y * 4 + x)]) for p in range(2)
+                ]
+            else:
+                pieces = [(bsrc.at[0, :, cols], dst.at[h, pl.ds(off + base_rows, 48)])]
+            for src, to in pieces:
+                cp = remote(src, to, s1_base.at[a, h], sem, {"grp": z, "seq": s, "rep": c})
+                if i:
+                    cp.start()
                 else:
-                    pieces = [(bsrc.at[0, :, cols], dst.at[h, pl.ds(off + base_rows, 48)])]
-                for src, to in pieces:
-                    cp = remote(src, to, s1_base.at[a, h], sem, {"grp": z, "seq": s, "rep": c})
-                    if i:
-                        cp.start()
-                    else:
-                        pl.when(yh == 1)(cp.start)
-                        pl.when(yh == 0)(pltpu.make_async_copy(src, to, sem).start)
-
-    stage1(0)
+                    pl.when(yh == 1)(cp.start)
+                    pl.when(yh == 0)(pltpu.make_async_copy(src, to, sem).start)
+
+    for a in range(3):
+        stage1(0, a)
     for cp in w_loc:
         cp.start()
 
@@ -150,37 +153,36 @@
         to = TXH + (OWN, 2 * OWN, 3 * OWN)[k]
         return remote(
             buf.at[h, pl.ds(lo, OWN)], buf.at[h, pl.ds(to, OWN)],
-            ex_send.at[i, h, k], ex_recv.at[i, h, k], (sib, dev_a, sib)[k],
+            ex_send.at[i, h, k], ex_recv.at[i, h, k], (sib, kv_dev[h], sib)[k],
         )
 
     def exchange_q(h):
-        return remote(Q.at[h, pl.ds(0, OWN)], Q.at[h, pl.ds(OWN, OWN)], q_send.at[h], q_recv.at[h], dev_b)
-
-    def pass_on(h):
-        wait_bytes(K.at[h, pl.ds(TXH, OWN)], s1_recv.at[0, h])
-        exchange(0, h, 1).start()
-        exchange(0, h, 0).start()
-        if h + 1 < NH:
-            stage1(h + 1)
-        wait_bytes(Q.at[h, pl.ds(0, OWN)], s1_recv.at[1, h])
-        exchange_q(h).start()
-        wait_bytes(V.at[h, pl.ds(TXH, OWN)], s1_recv.at[2, h])
-        exchange(1, h, 1).start()
-        exchange(1, h, 0).start()
-
-    def pass_second(h):
-        for i in range(2):
-            exchange(i, h, 1).wait_recv()
-            exchange(i, h, 2).start()
-
-    text_ok = lax.broadcasted_iota(jnp.int32, (ROWS, TXH), 1) + thalf * TXH < tl[0]
+        return remote(Q.at[h, pl.ds(0, OWN)], Q.at[h, pl.ds(OWN, OWN)], q_send.at[h], q_recv.at[h], q_dev[h])
+
+    def landed(h, a):
+        dst, off = arrays[a][2:]
+        wait_bytes(dst.at[h, pl.ds(off, OWN)], s1_recv.at[a, h])
+        if a == 0 and h + 1 < NH:
+            for i in range(3):
+                stage1(h + 1, i)
+        if a == 1:
+            exchange_q(h).start()
+        else:
+            exchange(a // 2, h, 1).start()
+            exchange(a // 2, h, 0).start()
+
+    def second(h, i):
+        exchange(i, h, 1).wait_recv()
+        exchange(i, h, 2).start()
+
+    text_at = lax.broadcasted_iota(jnp.int32, (ROWS, TXH), 1)
 
     def scores(h, r, size, lo, n):
         s = lax.dot_general(
             Q[h, pl.ds(r, size)], K[h, pl.ds(lo, n)], NT, preferred_element_type=jnp.float32
         )
         if lo == 0:
-            s = jnp.concatenate([jnp.where(text_ok, s[:, :TXH], -1e30), s[:, TXH:]], axis=1)
+            s = jnp.concatenate([jnp.where(text_at + thalf[h] * TXH < tl[0], s[:, :TXH], -1e30), s[:, TXH:]], axis=1)
         return s
 
     def fold(h, r, size, s, lo, n):
@@ -203,13 +205,19 @@
             L[h, rows] = part
             A[h, rows] = got
 
-    def tiles(h, todo, lo, n):
-        s = scores(h, *todo[0][:2], lo, n)
-        for i, (r, size, then) in enumerate(todo):
-            later = scores(h, *todo[i + 1][:2], lo, n) if i + 1 < len(todo) else None
-            fold(h, r, size, s, lo, n)
-            if then is not None:
-                then()
+    def tiles(todo):
+        def first(item):
+            h, b, r, size, before, _ = item
+            if before is not None:
+                before()
+            return scores(h, r, size, *BLOCK[b])
+
+        s = first(todo[0])
+        for i, (h, b, r, size, _, after) in enumerate(todo):
+            later = first(todo[i + 1]) if i + 1 < len(todo) else None
+            fold(h, r, size, s, *BLOCK[b])
+            if after is not None:
+                after()
             s = later
 
     def part_span(p):
@@ -218,9 +226,11 @@
     def send_part(h, p):
         rows = pl.ds(*part_span(p))
         return [
-            remote(PO.at[h, rows], RO.at[h, rows], p_send.at[0, h, p], p_recv.at[0, h, p], dev_b),
-            remote(PS.at[h, p], RS.at[h, p], p_send.at[1, h, p], p_recv.at[1, h, p], dev_b),
+            remote(PO.at[h, rows], RO.at[h, rows], p_send.at[0, h, p], p_recv.at[0, h, p], q_dev[h]),
+            remote(PS.at[h, p], RS.at[h, p], p_send.at[1, h, p], p_recv.at[1, h, p], q_dev[h]),
         ]
+
+    eye = lax.broadcasted_iota(jnp.int32, (HD, HD), 0) == lax.broadcasted_iota(jnp.int32, (HD, HD), 1)
 
     def log_sum(h, rows):
         total = jnp.broadcast_to(jnp.sum(L[h, rows], axis=1, keepdims=True), (HD, HD))
@@ -232,39 +242,30 @@
             rows = pl.ds(OWN + first + i * HD, HD)
             total, both = log_sum(h, rows)
             PO[h, pl.ds(first + i * HD, HD)] = (A[h, rows] / total).astype(jnp.bfloat16)
-            PS[h, p, pl.ds(i, 1)] = both.T[:1]
+            PS[h, p, pl.ds(i, 1)] = jnp.sum(jnp.where(eye, both, 0.0), axis=0, keepdims=True)
         for i in range(count // HD, 8):
             PS[h, p, pl.ds(i, 1)] = jnp.zeros((1, HD), jnp.float32)
         for cp in send_part(h, p):
             cp.start()
 
-    def phase_a(h):
+    def have_near(h):
         for i in range(2):
             exchange(i, h, 0).wait_recv()
             wait_bytes((K, V)[i].at[h, pl.ds(0, TXH)], loc.at[3 + i * NH + h])
-        near, far = [(0, ROWS, None), (ROWS, ROWS, None)], [(OWN, ROWS, None), (OWN + ROWS, ROWS, None)]
-        if h == 0:
-            tiles(h, near, 0, KA)
-            exchange_q(h).wait_recv()
-            tiles(h, far, 0, KA)
-        else:
-            exchange_q(h).wait_recv()
-            tiles(h, near + far, 0, KA)
-
-    def phase_b(h):
+
+    def have_far(h):
         for i in range(2):
             exchange(i, h, 2).wait_recv()
 
-        def over():
-            for p in range(2):
-                hand_over(h, p)
-
-        if h + 1 < NH:
-            todo = [(OWN, ROWS, None), (OWN + ROWS, ROWS, over), (0, ROWS, None), (ROWS, ROWS, None)]
-        else:
-            todo = [(OWN + part_span(p)[0], part_span(p)[1], lambda p=p: hand_over(h, p)) for p in range(2)]
-            todo += [(*part_span(p), None) for p in range(2)]
-        tiles(h, todo, KA, 2 * OWN)
+    def unit(h, b, far, before=None, mid=None, after=None):
+        r = far * OWN
+        return [(h, b, r, ROWS, before, mid), (h, b, r + ROWS, ROWS, None, after)]
+
+    def do(*steps):
+        def run():
+            for f, *args in steps:
+                f(*args)
+        return run
 
     OG = (OG0, OG1)
 
@@ -284,7 +285,8 @@
         for i in range(count // HD):
             rows = pl.ds(first + i * HD, HD)
             total, mine = log_sum(h, rows)
-            theirs = jnp.broadcast_to(RS[h, p, pl.ds(i, 1)], (HD, HD)).T
+            theirs = jnp.sum(jnp.where(eye, RS[h, p, pl.ds(i, 1)], 0.0), axis=1, keepdims=True)
+            theirs = jnp.broadcast_to(theirs, (HD, HD))
             top = jnp.maximum(mine, theirs)
             u, v = jnp.exp2(mine - top), jnp.exp2(theirs - top)
             value = A[h, rows] * (u / total) + RO[h, rows].astype(jnp.float32) * v
@@ -301,26 +303,38 @@
     w_sib = WX.at[pl.ds(pl.multiple_of((1 - yl) * 384 + (1 - c) * 192, 16), 192)]
     w_fwd = remote(w_got, w_got, w_send.at[1], w_recv.at[1], sib)
 
-    pass_on(0)
-    phase_a(0)
-    pass_on(1)
-    pass_second(0)
-    phase_b(0)
-    pass_on(2)
+    landed(0, 0)
+    landed(0, 1)
+    landed(0, 2)
+    have_near(0)
+    tiles(unit(0, 0, 0, mid=do((landed, 1, 0)), after=do((second, 0, 0))))
+    exchange_q(0).wait_recv()
+    tiles(unit(0, 0, 1, mid=do((landed, 1, 1)), after=do((second, 0, 1), (landed, 1, 2))))
+    have_far(0)
+    tiles(
+        unit(0, 1, 1, after=do((hand_over, 0, 0), (hand_over, 0, 1), (landed, 2, 0)))
+        + unit(1, 0, 0, before=do((have_near, 1)), after=do((landed, 2, 1)))
+        + unit(1, 0, 1, before=exchange_q(1).wait_recv, after=do((second, 1, 0)))
+        + unit(0, 1, 0, mid=do((landed, 2, 2)), after=do((second, 1, 1)))
+    )
     w_cp.start()
-    phase_a(1)
-    pass_second(1)
-    phase_b(1)
-    merge(0, 0)
-    merge(0, 1)
-    phase_a(2)
-    pass_second(2)
+    have_far(1)
+    tiles(
+        unit(1, 1, 1, after=do((hand_over, 1, 0), (hand_over, 1, 1)))
+        + unit(2, 0, 0, before=do((have_near, 2)), after=do((second, 2, 0)))
+        + unit(2, 0, 1, before=exchange_q(2).wait_recv, after=do((second, 2, 1)))
+        + unit(1, 1, 0, after=do((merge, 0, 0), (merge, 0, 1)))
+    )
+    have_far(2)
+    tiles(
+        [(2, 1, OWN + part_span(p)[0], part_span(p)[1], None, do((hand_over, 2, p))) for p in range(2)]
+        + [(2, 1, *part_span(p), None, None) for p in range(2)]
+    )
     wait_bytes(w_got, w_recv.at[0])
     w_fwd.start()
     merge(1, 0)
+    merge(2, 0)
     merge(1, 1)
-    phase_b(2)
-    merge(2, 0)
     merge(2, 1)
 
     S = ((SB0, SC0), (SB1, SC1))

time: 83.3 us -> 81.8 us (0.982); the launches traced: 82 us -> 81.6 us
  no operation moved by 1% of the time
where the time goes in v3:
time: 81.8 us; the launch traced here: 81.6 us
  Pallas kernels  78.6 us (96%)
  local copies, waits for them, and re-layouts  1.69 us (2%)
  between operations  1.31 us (2%)
    pallas_call x1, Pallas kernels, per_device(): pl.pallas_call(kernel, out_shape=jax.ShapeDtypeStruct((48, 3072), bf), in...  78.6 us
    unnamed x1, local copies, waits for them, and re-layouts  1.69 us

profile of v3, /device:TPU:0, one launch (start us, length us, event | category | flops | bytes accessed | tf_op | source)
XLA Modules:
  0.0 81.6 jit_solution(13993299286978821173)
XLA Ops:
  1.3 78.6 %shard_map.172 = bf16[48,3072]{1,0:T(8,128)(2,1)} custom-call(s32[1]{0:T(128)S(6)} %copy.21.tl, s32[1]{0:T(128)S(6)} %copy.20.ts, bf16[1,48,3072]{2,1,0:T(8,128)(2,1)} %bh.1, bf16[1,48,3072]{2,1,0:T(8,128)(2,1)} %bq.1, bf16[1,48,3072]{2,1,0:T(8,128)(2,1)} %bk.1, bf16[1,48,3072]{2,1,0:T(8,128)(2,1)} %bv.1, bf16[512,384]{1,0:T(8,128)(2,1)} %btk.1, ...), custom_call_target="tpu_custom_call" | custom-call | flops 10000000000 | bytes 30000000 | tf_op jit(solution)/shard_map/pallas_call | solution.py:422
  79.9 1.7 %copy.22 = bf16[1,48,3072]{2,1,0:T(8,128)(2,1)} copy(bf16[1,48,3072]{2,1,0:T(8,128)(2,1)} %bitcast.2) | data formatting | bytes 589824

commit v4 on v3

--- a/solution.py
+++ b/solution.py
@@ -18,6 +18,7 @@
 CH = 768
 C2 = math.log2(math.e) / math.sqrt(HD)
 BLOCK = ((0, KA), (KA, 2 * OWN))
+FAR_FIRST = (2, 1, 3)
 NT = (((1,), (1,)), ((), ()))
 MESH = pl.DeviceIdType.MESH
 
@@ -291,7 +292,7 @@
             u, v = jnp.exp2(mine - top), jnp.exp2(theirs - top)
             value = A[h, rows] * (u / total) + RO[h, rows].astype(jnp.float32) * v
             O[h, rows] = (value / (u + v)).astype(jnp.bfloat16)
-        for i in range(4):
+        for i in (*FAR_FIRST, 0):
             give(h, p, i).start()
 
     w_half = pl.ds(pl.multiple_of(c * 192, 16), 192)
@@ -362,12 +363,12 @@
             cols = pl.ds(n * CH, CH)
             got = jnp.dot(OG[p][0], WX[:, cols], preferred_element_type=jnp.float32)
             S[p][0][:, cols] = (GT[step, 0:1, cols] * got).astype(jnp.bfloat16)
-            for i in range(1, 4):
+            for i in FAR_FIRST:
                 scatter(p, 0, n, i).start()
             got = GT[step, 1:2, cols] * jnp.dot(OG[p][1], WC[:, cols], preferred_element_type=jnp.float32)
             got = got + jnp.where(z == n, hidden, 0.0)
             S[p][1][:, cols] = (gain[0:1, cols] * got).astype(jnp.bfloat16)
-            for i in range(1, 4):
+            for i in FAR_FIRST:
                 scatter(p, 1, n, i).start()
     for p in range(2):
         first, count = PARTS[p]

time: 81.8 us -> 81.2 us (level)
  no operation moved by 1% of the time
where the time goes in v4:
time: 81.2 us; the launch traced here: 80.9 us
  Pallas kernels  77.9 us (96%)
  local copies, waits for them, and re-layouts  1.69 us (2%)
  between operations  1.31 us (2%)
    pallas_call x1, Pallas kernels, per_device(): pl.pallas_call(kernel, out_shape=jax.ShapeDtypeStruct((48, 3072), bf), in...  77.9 us
    unnamed x1, local copies, waits for them, and re-layouts  1.69 us

profile of v4, /device:TPU:0, one launch (start us, length us, event | category | flops | bytes accessed | tf_op | source)
XLA Modules:
  0.0 80.9 jit_solution(142700794487998677)
XLA Ops:
  1.3 77.9 %shard_map.172 = bf16[48,3072]{1,0:T(8,128)(2,1)} custom-call(s32[1]{0:T(128)S(6)} %copy.21.tl, s32[1]{0:T(128)S(6)} %copy.20.ts, bf16[1,48,3072]{2,1,0:T(8,128)(2,1)} %bh.1, bf16[1,48,3072]{2,1,0:T(8,128)(2,1)} %bq.1, bf16[1,48,3072]{2,1,0:T(8,128)(2,1)} %bk.1, bf16[1,48,3072]{2,1,0:T(8,128)(2,1)} %bv.1, bf16[512,384]{1,0:T(8,128)(2,1)} %btk.1, ...), custom_call_target="tpu_custom_call" | custom-call | flops 10000000000 | bytes 30000000 | tf_op jit(solution)/shard_map/pallas_call | solution.py:423
  79.2 1.7 %copy.22 = bf16[1,48,3072]{2,1,0:T(8,128)(2,1)} copy(bf16[1,48,3072]{2,1,0:T(8,128)(2,1)} %bitcast.2) | data formatting | bytes 589824
